TPU v7x, 32 devices: a whole 2x2x4 slice. The times are simulated.
32 devices in a mesh: gx: 2 (over y), gy: 4 (over z), gz: 4 (over x, core).
Axes of the slice: x: 2, y: 2, z: 4, core: 2. Of those that a mesh axis runs over, the one named last changes fastest.
Arguments:
- views: float32 [6, 16, 64, 512], P(None, 'gx', ('gy', 'gz')), may hold values from 0.2 to 5
- estimate: float32 [16, 64, 512], P('gx', 'gy', 'gz'), may hold values from 0.5 to 2
- psf: float32 [6, 3, 17], replicated, may hold values from 0.2 to 1
- extents: int32 [6, 3, 2], replicated, may hold values from 0 to 512, as said below
Outputs:
- deconvolved: float32 [16, 64, 512], P('gx', 'gy', 'gz')
Inputs may be any that keep to these rules, and one draw needn't show every extreme that they name: extents[v, a, 0] < extents[v, a, 1] <= the number of cells along axis a (16, 64, 512 for a = 0, 1, 2).
All inputs are finite; a program needn't handle non-finite values.
Results may differ from a plain program's by a relative error of at most 0.0003.
Values sent between devices are 32-bit elements; how exact they have to be, the bound alone decides.
A program may use at most 64 MiB of HBM per device.

v0:
```python
import jax
import jax.numpy as jnp
from jax import lax
from jax.sharding import PartitionSpec as P

H = 8
K = 17
ITERS = 2


def padded_2(array, sides, width):
    for axis, dim in sides:
        devices, length = (lax.axis_size(axis), array.shape[dim])
        up = [(i, (i + 1) % devices) for i in range(devices - 1)]
        down = [(j, i) for i, j in up]
        last = lax.slice_in_dim(array, length - width, length, axis=dim)
        leading = lax.slice_in_dim(array, 0, width, axis=dim)
        before = lax.ppermute(last, axis, up)
        after = lax.ppermute(leading, axis, down)
        array = jnp.concatenate([before, array, after], axis=dim)
    return array


def band_matrix(kernels, length):
    rows = length + 2 * H
    offset = (
        jnp.arange(rows, dtype=jnp.int32)[:, None] - jnp.arange(length, dtype=jnp.int32)[None, :]
    )
    picks = (offset[:, :, None] == jnp.arange(K, dtype=jnp.int32)[None, None, :]).astype(
        jnp.float32
    )
    return jnp.einsum("ijt,vt->vij", picks, kernels, precision=lax.Precision.HIGHEST)


def blur_along(padded, kernels, axis, length):
    matrix = band_matrix(kernels, length)
    source = "vxyz" if padded.shape[0] == kernels.shape[0] else "uxyz"
    letter = "vxyz"[axis]
    target = "vxyz".replace(letter, "a")
    form = source + ",v" + letter + "a->" + target
    return jnp.einsum(form, padded, matrix, precision=lax.Precision.HIGHEST)


def blur_padded(padded, kernels, sides):
    result = padded
    for axis in range(3):
        result = blur_along(result, kernels[:, axis], axis + 1, sides[axis])
    return result


def view_weights(extents, sides):
    first = lax.axis_index("gx") * sides[0] + jnp.arange(sides[0], dtype=jnp.int32)
    second = lax.axis_index("gy") * sides[1] + jnp.arange(sides[1], dtype=jnp.int32)
    third = lax.axis_index("gz") * sides[2] + jnp.arange(sides[2], dtype=jnp.int32)
    inside_first = (first[None, :] >= extents[:, 0, 0:1]) & (first[None, :] < extents[:, 0, 1:2])
    inside_second = (second[None, :] >= extents[:, 1, 0:1]) & (second[None, :] < extents[:, 1, 1:2])
    inside_third = (third[None, :] >= extents[:, 2, 0:1]) & (third[None, :] < extents[:, 2, 1:2])
    inside = (
        inside_first[:, :, None, None]
        & inside_second[:, None, :, None]
        & inside_third[:, None, None, :]
    )
    return jnp.where(inside, jnp.float32(1.0), jnp.float32(0.25))


def shards(views, estimate, psf, extents):
    images = lax.all_to_all(views, "gz", split_axis=3, concat_axis=2, tiled=True)
    sides = estimate.shape
    taps = psf / jnp.sum(psf, axis=-1, keepdims=True)
    flipped = taps[:, :, ::-1]
    weights = view_weights(extents, sides)
    weight_sum = jnp.sum(weights, axis=0)
    deconvolved = estimate
    for step in range(ITERS):
        padded = padded_2(deconvolved, (("gx", 0), ("gy", 1), ("gz", 2)), H)
        blurred = blur_padded(padded[None], taps, sides)
        ratio = images / blurred
        ratio_padded = padded_2(ratio, (("gx", 1), ("gy", 2), ("gz", 3)), H)
        back = blur_padded(ratio_padded, flipped, sides)
        summed = jnp.sum(weights * back, axis=0)
        deconvolved = deconvolved * (summed / weight_sum)
    return deconvolved


def solution(mesh):
    placed = (P(None, "gx", ("gy", "gz"), None), P("gx", "gy", "gz"), P(), P())
    return jax.shard_map(
        shards, mesh=mesh, in_specs=placed, out_specs=P("gx", "gy", "gz"), check_vma=False
    )
```

profile of v0, /device:TPU:1, one launch (start us, length us, event | category | flops | bytes accessed | tf_op | source)
XLA Modules:
  0.0 237.1 jit_solution(14778438990561085680)
XLA Ops:
  0.9 4.0 %collective-permute-start = (f32[8,16,128]{2,0,1:T(8,128)S(1)}, f32[8,16,128]{2,0,1:T(8,128)S(1)}, u32[]{:S(2)}, u32[]{:S(2)}) collective-permute-start(f32[8,16,128]{2,0,1:T(8,128)S(1)} %copy.81), channel_id=1, source_target_pairs={{0,16},{1,17},{2,18},{3,19},{4,20},{5,21},{6,22},{7,23},{8,24},{9,... | collective-permute-start | bytes 196616 | tf_op jit(solution)/shard_map/ppermute | solution.py:18
  6.1 5.9 %copy.62 = f32[6,8,4,512]{1,2,0,3:T(4,128)} copy(f32[6,8,4,512]{3,2,1,0:T(4,128)} %param.4) | data formatting | bytes 786432 | tf_op args[0]
  12.1 9.2 %reshape.251 = f32[4,1,24576]{2,1,0:T(1,128)} reshape(f32[512,6,4,8]{3,2,1,0:T(4,128)} %bitcast.82) | data formatting | bytes 786432
  21.3 4.4 %all-to-all-start = ((f32[4,1,24576]{2,1,0:T(1,128)}), f32[4,1,24576]{2,1,0:T(1,128)S(1)}, u32[]{:S(2)}, u32[]{:S(2)}) async-start(f32[4,1,24576]{2,1,0:T(1,128)} %reshape.251), calls=%async_computation | async-start | bytes 786432 | tf_op jit(solution)/shard_map/all_to_all | solution.py:67
  33.3 3.8 %collective-permute-done.3 = f32[24,8,128]{2,0,1:T(8,128)S(1)} collective-permute-done((f32[24,8,128]{2,0,1:T(8,128)S(1)}, f32[24,8,128]{2,0,1:T(8,128)S(1)}, u32[]{:S(2)}, u32[]{:S(2)}) %collective-permute-start.3) | collective-permute-done | bytes 98336 | tf_op jit(solution)/shard_map/ppermute | solution.py:19
  37.3 4.4 %collective-permute-start.4 = (f32[24,32,8]{2,0,1:T(8,128)S(1)}, f32[24,32,8]{2,0,1:T(8,128)S(1)}, u32[]{:S(2)}, u32[]{:S(2)}) collective-permute-start(f32[24,32,8]{2,0,1:T(8,128)S(1)} %get-tuple-element.15), channel_id=1, source_target_pairs={{0,1},{1,2},{2,3},{4,5},{5,6},{6,7},{8,9},{9,10},{10,11},{12,13},{... | collective-permute-start | bytes 73736 | tf_op jit(solution)/shard_map/ppermute | solution.py:18
  46.4 4.4 %collective-permute-done.5 = f32[24,32,8]{2,0,1:T(8,128)S(1)} collective-permute-done((f32[24,32,8]{2,0,1:T(8,128)S(1)}, f32[24,32,8]{2,0,1:T(8,128)S(1)}, u32[]{:S(2)}, u32[]{:S(2)}) %collective-permute-start.5) | collective-permute-done | bytes 24608 | tf_op jit(solution)/shard_map/ppermute | solution.py:19
  56.5 10.2 %reshape.252 = f32[512,6,4,8]{3,2,1,0:T(4,128)} reshape(f32[4,24576]{1,0:T(4,128)S(1)} %reduce) | data formatting | bytes 786432
  66.7 5.1 %copy.63 = f32[6,8,4,4,128]{4,2,3,1,0:T(4,128)S(1)} copy(f32[6,8,4,4,128]{1,2,0,4,3:T(4,128)} %bitcast.81) | data formatting | bytes 786432 | tf_op jit(solution)/shard_map/all_to_all | solution.py:67
  72.7 4.3 %collective-permute-start.6 = (f32[6,8,16,128]{3,2,1,0:T(8,128)S(1)}, f32[6,8,16,128]{3,2,1,0:T(8,128)S(1)}, u32[]{:S(2)}, u32[]{:S(2)}) collective-permute-start(f32[6,8,16,128]{3,2,1,0:T(8,128)S(1)} %convolution_divide_fusion.1), channel_id=1, source_target_pairs={{0,16},{1,17},{2,18},{3,19},{4,20},{5,21},{6,22},{7,23},{8,24},{9,... | collective-permute-start | bytes 1179656 | tf_op jit(solution)/shard_map/ppermute | solution.py:18
  81.7 3.8 %collective-permute-done.7 = f32[6,8,16,128]{3,2,1,0:T(8,128)S(1)} collective-permute-done((f32[6,8,16,128]{3,2,1,0:T(8,128)S(1)}, f32[6,8,16,128]{3,2,1,0:T(8,128)S(1)}, u32[]{:S(2)}, u32[]{:S(2)}) %collective-permute-start.7) | collective-permute-done | bytes 393248 | tf_op jit(solution)/shard_map/ppermute | solution.py:19
  92.1 7.5 %collective-permute-done.8 = f32[6,24,8,128]{3,2,1,0:T(8,128)S(1)} collective-permute-done((f32[6,24,8,128]{3,2,1,0:T(8,128)}, f32[6,24,8,128]{3,2,1,0:T(8,128)S(1)}, u32[]{:S(2)}, u32[]{:S(2)}) %collective-permute-start.8) | collective-permute-done | bytes 589856 | tf_op jit(solution)/shard_map/ppermute | solution.py:18
  99.6 3.8 %collective-permute-done.9 = f32[6,24,8,128]{3,2,1,0:T(8,128)S(1)} collective-permute-done((f32[6,24,8,128]{3,2,1,0:T(8,128)S(1)}, f32[6,24,8,128]{3,2,1,0:T(8,128)S(1)}, u32[]{:S(2)}, u32[]{:S(2)}) %collective-permute-start.9) | collective-permute-done | bytes 589856 | tf_op jit(solution)/shard_map/ppermute | solution.py:19
  120.8 4.1 %collective-permute-done.11 = f32[6,24,32,8]{2,3,1,0:T(8,128)} collective-permute-done((f32[6,24,32,8]{2,3,1,0:T(8,128)}, f32[6,24,32,8]{2,3,1,0:T(8,128)}, u32[]{:S(2)}, u32[]{:S(2)}) %collective-permute-start.11) | collective-permute-done | bytes 147488 | tf_op jit(solution)/shard_map/ppermute | solution.py:19
  128.1 4.9 %pad_maximum_fusion = f32[6,24,32,144]{3,2,1,0:T(8,128)S(1)} fusion(f32[6,24,32,8]{3,2,1,0:T(8,128)} %copy.73, f32[6,24,8,128]{3,2,1,0:T(8,128)} %copy-done.9, f32[6,8,16,128]{3,2,1,0:T(8,128)} %copy-done.3, f32[6,8,16,128]{3,2,1,0:T(8,128)S(1)} %convolution_divide_fusion.1, f32[6,8,16,128]{3,2,1,0:T(8,128)} %copy-done.2, f32[6,24,8,128]{3,2,1,0:T(8,128)} %copy-done.8, ...), kind=kLoop, calls=%fused_computation | loop fusion | flops 3981312 | bytes 5308416 | tf_op jit(solution)/shard_map/concatenate | solution.py:20
  133.0 5.2 %fusion.2 = f32[6,8,32,144]{3,1,2,0:T(8,128)S(1)} fusion(f32[6,24,32,144]{3,2,1,0:T(8,128)S(1)} %pad_maximum_fusion, f32[6,24,8,1]{1,0,2,3:T(8,128)S(1)} %copy-done.19), kind=kOutput, calls=%fused_computation.4 | convolution fusion | flops 63700992 | bytes 3543552 | tf_op jit(solution)/shard_map/vxyz,vxa->vayz/dot_general | solution.py:41
  155.7 4.5 %collective-permute-start.16 = (f32[24,32,8]{2,0,1:T(8,128)S(1)}, f32[24,32,8]{2,0,1:T(8,128)S(1)}, u32[]{:S(2)}, u32[]{:S(2)}) collective-permute-start(f32[24,32,8]{2,0,1:T(8,128)S(1)} %get-tuple-element.13), channel_id=1, source_target_pairs={{0,1},{1,2},{2,3},{4,5},{5,6},{6,7},{8,9},{9,10},{10,11},{12,13},{... | collective-permute-start | bytes 73736 | tf_op jit(solution)/shard_map/ppermute | solution.py:18
  164.9 4.5 %collective-permute-done.17 = f32[24,32,8]{2,0,1:T(8,128)S(1)} collective-permute-done((f32[24,32,8]{2,0,1:T(8,128)S(1)}, f32[24,32,8]{2,0,1:T(8,128)S(1)}, u32[]{:S(2)}, u32[]{:S(2)}) %collective-permute-start.17) | collective-permute-done | bytes 24608 | tf_op jit(solution)/shard_map/ppermute | solution.py:19
  179.7 3.8 %collective-permute-done.19 = f32[6,8,16,128]{3,2,1,0:T(8,128)S(1)} collective-permute-done((f32[6,8,16,128]{3,2,1,0:T(8,128)S(1)}, f32[6,8,16,128]{3,2,1,0:T(8,128)S(1)}, u32[]{:S(2)}, u32[]{:S(2)}) %collective-permute-start.19) | collective-permute-done | bytes 393248 | tf_op jit(solution)/shard_map/ppermute | solution.py:19
  186.8 8.2 %collective-permute-done.20 = f32[6,24,8,128]{3,2,1,0:T(8,128)S(1)} collective-permute-done((f32[6,24,8,128]{3,2,1,0:T(8,128)S(1)}, f32[6,24,8,128]{3,2,1,0:T(8,128)S(1)}, u32[]{:S(2)}, u32[]{:S(2)}) %collective-permute-start.20) | collective-permute-done | bytes 589856 | tf_op jit(solution)/shard_map/ppermute | solution.py:18
  195.0 4.1 %collective-permute-done.21 = f32[6,24,8,128]{3,2,1,0:T(8,128)S(1)} collective-permute-done((f32[6,24,8,128]{3,2,1,0:T(8,128)S(1)}, f32[6,24,8,128]{3,2,1,0:T(8,128)S(1)}, u32[]{:S(2)}, u32[]{:S(2)}) %collective-permute-start.21) | collective-permute-done | bytes 589856 | tf_op jit(solution)/shard_map/ppermute | solution.py:19
  216.5 4.1 %collective-permute-done.23 = f32[6,24,32,8]{2,3,1,0:T(8,128)} collective-permute-done((f32[6,24,32,8]{2,3,1,0:T(8,128)}, f32[6,24,32,8]{2,3,1,0:T(8,128)}, u32[]{:S(2)}, u32[]{:S(2)}) %collective-permute-start.23) | collective-permute-done | bytes 147488 | tf_op jit(solution)/shard_map/ppermute | solution.py:19
  223.8 4.9 %pad_maximum_fusion.1 = f32[6,24,32,144]{3,2,1,0:T(8,128)S(1)} fusion(f32[6,24,32,8]{3,2,1,0:T(8,128)} %copy.88, f32[6,24,8,128]{3,2,1,0:T(8,128)} %copy-done.11, f32[6,8,16,128]{3,2,1,0:T(8,128)} %copy-done.5, f32[6,8,16,128]{3,2,1,0:T(8,128)S(1)} %convolution_divide_fusion, f32[6,8,16,128]{3,2,1,0:T(8,128)} %copy-done.4, f32[6,24,8,128]{3,2,1,0:T(8,128)} %copy-done.10, ...), kind=kLoop, calls=%fused_computation.1 | loop fusion | flops 3981312 | bytes 5308416 | tf_op jit(solution)/shard_map/concatenate | solution.py:20
  228.7 5.2 %fusion = f32[6,8,32,144]{3,1,2,0:T(8,128)S(1)} fusion(f32[6,24,32,144]{3,2,1,0:T(8,128)S(1)} %pad_maximum_fusion.1, f32[6,24,8,1]{1,0,2,3:T(8,128)S(1)} %copy-done.20), kind=kOutput, calls=%fused_computation.2 | convolution fusion | flops 63700992 | bytes 3543552 | tf_op jit(solution)/shard_map/vxyz,vxa->vayz/dot_general | solution.py:41
  (161 shorter events, 111.5 us)
Async XLA Ops:
  0.9 26.9 %collective-permute-start = (f32[8,16,128]{2,0,1:T(8,128)S(1)}, f32[8,16,128]{2,0,1:T(8,128)S(1)}, u32[]{:S(2)}, u32[]{:S(2)}) collective-permute-start(f32[8,16,128]{2,0,1:T(8,128)S(1)} %copy.81), channel_id=1, source_target_pairs={{0,16},{1,17},{2,18},{3,19},{4,20},{5,21},{6,22},{7,23},{8,24},{9,... | collective-permute-start | bytes 196616 | tf_op jit(solution)/shard_map/ppermute | solution.py:18
  4.8 23.0 %collective-permute-start.1 = (f32[8,16,128]{2,0,1:T(8,128)S(1)}, f32[8,16,128]{2,0,1:T(8,128)S(1)}, u32[]{:S(2)}, u32[]{:S(2)}) collective-permute-start(f32[8,16,128]{2,0,1:T(8,128)S(1)} %copy.81), channel_id=1, source_target_pairs={{16,0},{17,1},{18,2},{19,3},{20,4},{21,5},{22,6},{23,7},{24,8},{25... | collective-permute-start | bytes 196616 | tf_op jit(solution)/shard_map/ppermute | solution.py:19
  21.3 32.9 %all-to-all-start = ((f32[4,1,24576]{2,1,0:T(1,128)}), f32[4,1,24576]{2,1,0:T(1,128)S(1)}, u32[]{:S(2)}, u32[]{:S(2)}) async-start(f32[4,1,24576]{2,1,0:T(1,128)} %reshape.251), calls=%async_computation | async-start | bytes 786432 | tf_op jit(solution)/shard_map/all_to_all | solution.py:67
  27.9 5.4 %collective-permute-start.2 = (f32[24,8,128]{2,0,1:T(8,128)S(1)}, f32[24,8,128]{2,0,1:T(8,128)S(1)}, u32[]{:S(2)}, u32[]{:S(2)}) collective-permute-start(f32[24,8,128]{2,0,1:T(8,128)S(1)} %get-tuple-element.19), channel_id=1, source_target_pairs={{0,4},{4,8},{8,12},{1,5},{5,9},{9,13},{2,6},{6,10},{10,14},{3,7},{... | collective-permute-start | bytes 294920 | tf_op jit(solution)/shard_map/ppermute | solution.py:18
  31.1 5.9 %collective-permute-start.3 = (f32[24,8,128]{2,0,1:T(8,128)S(1)}, f32[24,8,128]{2,0,1:T(8,128)S(1)}, u32[]{:S(2)}, u32[]{:S(2)}) collective-permute-start(f32[24,8,128]{2,0,1:T(8,128)S(1)} %get-tuple-element.20), channel_id=1, source_target_pairs={{4,0},{8,4},{12,8},{5,1},{9,5},{13,9},{6,2},{10,6},{14,10},{7,3},{... | collective-permute-start | bytes 294920 | tf_op jit(solution)/shard_map/ppermute | solution.py:19
  37.3 9.1 %collective-permute-start.4 = (f32[24,32,8]{2,0,1:T(8,128)S(1)}, f32[24,32,8]{2,0,1:T(8,128)S(1)}, u32[]{:S(2)}, u32[]{:S(2)}) collective-permute-start(f32[24,32,8]{2,0,1:T(8,128)S(1)} %get-tuple-element.15), channel_id=1, source_target_pairs={{0,1},{1,2},{2,3},{4,5},{5,6},{6,7},{8,9},{9,10},{10,11},{12,13},{... | collective-permute-start | bytes 73736 | tf_op jit(solution)/shard_map/ppermute | solution.py:18
  41.7 9.1 %collective-permute-start.5 = (f32[24,32,8]{2,0,1:T(8,128)S(1)}, f32[24,32,8]{2,0,1:T(8,128)S(1)}, u32[]{:S(2)}, u32[]{:S(2)}) collective-permute-start(f32[24,32,8]{2,0,1:T(8,128)S(1)} %get-tuple-element.16), channel_id=1, source_target_pairs={{1,0},{2,1},{3,2},{5,4},{6,5},{7,6},{9,8},{10,9},{11,10},{13,12},{... | collective-permute-start | bytes 73736 | tf_op jit(solution)/shard_map/ppermute | solution.py:19
  72.7 9.0 %collective-permute-start.6 = (f32[6,8,16,128]{3,2,1,0:T(8,128)S(1)}, f32[6,8,16,128]{3,2,1,0:T(8,128)S(1)}, u32[]{:S(2)}, u32[]{:S(2)}) collective-permute-start(f32[6,8,16,128]{3,2,1,0:T(8,128)S(1)} %convolution_divide_fusion.1), channel_id=1, source_target_pairs={{0,16},{1,17},{2,18},{3,19},{4,20},{5,21},{6,22},{7,23},{8,24},{9,... | collective-permute-start | bytes 1179656 | tf_op jit(solution)/shard_map/ppermute | solution.py:18
  77.0 8.5 %collective-permute-start.7 = (f32[6,8,16,128]{3,2,1,0:T(8,128)S(1)}, f32[6,8,16,128]{3,2,1,0:T(8,128)S(1)}, u32[]{:S(2)}, u32[]{:S(2)}) collective-permute-start(f32[6,8,16,128]{3,2,1,0:T(8,128)S(1)} %convolution_divide_fusion.1), channel_id=1, source_target_pairs={{16,0},{17,1},{18,2},{19,3},{20,4},{21,5},{22,6},{23,7},{24,8},{25... | collective-permute-start | bytes 1179656 | tf_op jit(solution)/shard_map/ppermute | solution.py:19
  86.6 13.1 %collective-permute-start.8 = (f32[6,24,8,128]{3,2,1,0:T(8,128)}, f32[6,24,8,128]{3,2,1,0:T(8,128)S(1)}, u32[]{:S(2)}, u32[]{:S(2)}) collective-permute-start(f32[6,24,8,128]{3,2,1,0:T(8,128)} %get-tuple-element.11), channel_id=1, source_target_pairs={{0,4},{4,8},{8,12},{1,5},{5,9},{9,13},{2,6},{6,10},{10,14},{3,7},{... | collective-permute-start | bytes 1769480 | tf_op jit(solution)/shard_map/ppermute | solution.py:18
  89.8 13.7 %collective-permute-start.9 = (f32[6,24,8,128]{3,2,1,0:T(8,128)S(1)}, f32[6,24,8,128]{3,2,1,0:T(8,128)S(1)}, u32[]{:S(2)}, u32[]{:S(2)}) collective-permute-start(f32[6,24,8,128]{3,2,1,0:T(8,128)S(1)} %get-tuple-element.12), channel_id=1, source_target_pairs={{4,0},{8,4},{12,8},{5,1},{9,5},{13,9},{6,2},{10,6},{14,10},{7,3},{... | collective-permute-start | bytes 1769480 | tf_op jit(solution)/shard_map/ppermute | solution.py:19
  110.0 9.0 %collective-permute-start.10 = (f32[6,24,32,8]{2,3,1,0:T(8,128)}, f32[6,24,32,8]{2,3,1,0:T(8,128)}, u32[]{:S(2)}, u32[]{:S(2)}) collective-permute-start(f32[6,24,32,8]{2,3,1,0:T(8,128)} %copy.70), channel_id=1, source_target_pairs={{0,1},{1,2},{2,3},{4,5},{5,6},{6,7},{8,9},{9,10},{10,11},{12,13},{... | collective-permute-start | bytes 442376 | tf_op jit(solution)/shard_map/ppermute | solution.py:18
  113.4 11.5 %collective-permute-start.11 = (f32[6,24,32,8]{2,3,1,0:T(8,128)}, f32[6,24,32,8]{2,3,1,0:T(8,128)}, u32[]{:S(2)}, u32[]{:S(2)}) collective-permute-start(f32[6,24,32,8]{2,3,1,0:T(8,128)} %copy.71), channel_id=1, source_target_pairs={{1,0},{2,1},{3,2},{5,4},{6,5},{7,6},{9,8},{10,9},{11,10},{13,12},{... | collective-permute-start | bytes 442376 | tf_op jit(solution)/shard_map/ppermute | solution.py:19
  141.9 5.0 %collective-permute-start.13 = (f32[8,16,128]{2,0,1:T(8,128)S(1)}, f32[8,16,128]{2,0,1:T(8,128)S(1)}, u32[]{:S(2)}, u32[]{:S(2)}) collective-permute-start(f32[8,16,128]{2,0,1:T(8,128)S(1)} %fusion.61), channel_id=1, source_target_pairs={{16,0},{17,1},{18,2},{19,3},{20,4},{21,5},{22,6},{23,7},{24,8},{25... | collective-permute-start | bytes 196616 | tf_op jit(solution)/shard_map/ppermute | solution.py:19
  146.9 4.8 %collective-permute-start.14 = (f32[24,8,128]{2,0,1:T(8,128)S(1)}, f32[24,8,128]{2,0,1:T(8,128)S(1)}, u32[]{:S(2)}, u32[]{:S(2)}) collective-permute-start(f32[24,8,128]{2,0,1:T(8,128)S(1)} %get-tuple-element.17), channel_id=1, source_target_pairs={{0,4},{4,8},{8,12},{1,5},{5,9},{9,13},{2,6},{6,10},{10,14},{3,7},{... | collective-permute-start | bytes 294920 | tf_op jit(solution)/shard_map/ppermute | solution.py:18
  150.1 5.4 %collective-permute-start.15 = (f32[24,8,128]{2,0,1:T(8,128)S(1)}, f32[24,8,128]{2,0,1:T(8,128)S(1)}, u32[]{:S(2)}, u32[]{:S(2)}) collective-permute-start(f32[24,8,128]{2,0,1:T(8,128)S(1)} %get-tuple-element.18), channel_id=1, source_target_pairs={{4,0},{8,4},{12,8},{5,1},{9,5},{13,9},{6,2},{10,6},{14,10},{7,3},{... | collective-permute-start | bytes 294920 | tf_op jit(solution)/shard_map/ppermute | solution.py:19
  155.7 9.2 %collective-permute-start.16 = (f32[24,32,8]{2,0,1:T(8,128)S(1)}, f32[24,32,8]{2,0,1:T(8,128)S(1)}, u32[]{:S(2)}, u32[]{:S(2)}) collective-permute-start(f32[24,32,8]{2,0,1:T(8,128)S(1)} %get-tuple-element.13), channel_id=1, source_target_pairs={{0,1},{1,2},{2,3},{4,5},{5,6},{6,7},{8,9},{9,10},{10,11},{12,13},{... | collective-permute-start | bytes 73736 | tf_op jit(solution)/shard_map/ppermute | solution.py:18
  160.2 9.2 %collective-permute-start.17 = (f32[24,32,8]{2,0,1:T(8,128)S(1)}, f32[24,32,8]{2,0,1:T(8,128)S(1)}, u32[]{:S(2)}, u32[]{:S(2)}) collective-permute-start(f32[24,32,8]{2,0,1:T(8,128)S(1)} %get-tuple-element.14), channel_id=1, source_target_pairs={{1,0},{2,1},{3,2},{5,4},{6,5},{7,6},{9,8},{10,9},{11,10},{13,12},{... | collective-permute-start | bytes 73736 | tf_op jit(solution)/shard_map/ppermute | solution.py:19
  173.7 6.0 %collective-permute-start.18 = (f32[6,8,16,128]{3,2,1,0:T(8,128)S(1)}, f32[6,8,16,128]{3,2,1,0:T(8,128)S(1)}, u32[]{:S(2)}, u32[]{:S(2)}) collective-permute-start(f32[6,8,16,128]{3,2,1,0:T(8,128)S(1)} %convolution_divide_fusion), channel_id=1, source_target_pairs={{0,16},{1,17},{2,18},{3,19},{4,20},{5,21},{6,22},{7,23},{8,24},{9,... | collective-permute-start | bytes 1179656 | tf_op jit(solution)/shard_map/ppermute | solution.py:18
  175.1 8.5 %collective-permute-start.19 = (f32[6,8,16,128]{3,2,1,0:T(8,128)S(1)}, f32[6,8,16,128]{3,2,1,0:T(8,128)S(1)}, u32[]{:S(2)}, u32[]{:S(2)}) collective-permute-start(f32[6,8,16,128]{3,2,1,0:T(8,128)S(1)} %convolution_divide_fusion), channel_id=1, source_target_pairs={{16,0},{17,1},{18,2},{19,3},{20,4},{21,5},{22,6},{23,7},{24,8},{25... | collective-permute-start | bytes 1179656 | tf_op jit(solution)/shard_map/ppermute | solution.py:19
  183.8 11.2 %collective-permute-start.20 = (f32[6,24,8,128]{3,2,1,0:T(8,128)S(1)}, f32[6,24,8,128]{3,2,1,0:T(8,128)S(1)}, u32[]{:S(2)}, u32[]{:S(2)}) collective-permute-start(f32[6,24,8,128]{3,2,1,0:T(8,128)S(1)} %get-tuple-element.9), channel_id=1, source_target_pairs={{0,4},{4,8},{8,12},{1,5},{5,9},{9,13},{2,6},{6,10},{10,14},{3,7},{... | collective-permute-start | bytes 1769480 | tf_op jit(solution)/shard_map/ppermute | solution.py:18
  185.5 13.6 %collective-permute-start.21 = (f32[6,24,8,128]{3,2,1,0:T(8,128)S(1)}, f32[6,24,8,128]{3,2,1,0:T(8,128)S(1)}, u32[]{:S(2)}, u32[]{:S(2)}) collective-permute-start(f32[6,24,8,128]{3,2,1,0:T(8,128)S(1)} %get-tuple-element.10), channel_id=1, source_target_pairs={{4,0},{8,4},{12,8},{5,1},{9,5},{13,9},{6,2},{10,6},{14,10},{7,3},{... | collective-permute-start | bytes 1769480 | tf_op jit(solution)/shard_map/ppermute | solution.py:19
  205.7 9.0 %collective-permute-start.22 = (f32[6,24,32,8]{2,3,1,0:T(8,128)}, f32[6,24,32,8]{2,3,1,0:T(8,128)}, u32[]{:S(2)}, u32[]{:S(2)}) collective-permute-start(f32[6,24,32,8]{2,3,1,0:T(8,128)} %copy.85), channel_id=1, source_target_pairs={{0,1},{1,2},{2,3},{4,5},{5,6},{6,7},{8,9},{9,10},{10,11},{12,13},{... | collective-permute-start | bytes 442376 | tf_op jit(solution)/shard_map/ppermute | solution.py:18
  209.1 11.5 %collective-permute-start.23 = (f32[6,24,32,8]{2,3,1,0:T(8,128)}, f32[6,24,32,8]{2,3,1,0:T(8,128)}, u32[]{:S(2)}, u32[]{:S(2)}) collective-permute-start(f32[6,24,32,8]{2,3,1,0:T(8,128)} %copy.86), channel_id=1, source_target_pairs={{1,0},{2,1},{3,2},{5,4},{6,5},{7,6},{9,8},{10,9},{11,10},{13,12},{... | collective-permute-start | bytes 442376 | tf_op jit(solution)/shard_map/ppermute | solution.py:19
  (31 other events, 365.0 us)
where the time goes:
time: 242 us; the launch traced here: 237 us
  waiting for transfers between devices  74 us (31%)
  local copies, waits for them, and re-layouts  61.1 us (25%)
  starting transfers between devices  60.9 us (25%)
  matrix products  27 us (11%)
  other arithmetic  13 us (5%)
    ppermute x12, waiting for transfers between devices, padded_2(): after = lax.ppermute(leading, axis, down)  44.1 us
    ppermute x12, starting transfers between devices, padded_2(): before = lax.ppermute(last, axis, up)  34.8 us
    ppermute x12, waiting for transfers between devices, padded_2(): before = lax.ppermute(last, axis, up)  30 us
    unnamed x66, local copies, waits for them, and re-layouts  28.1 us
    dot_general x12, matrix products, blur_along(): return jnp.einsum(form, padded, matrix, precision=lax.Precision.HIGHEST)  23.3 us
    ppermute x12, starting transfers between devices, padded_2(): after = lax.ppermute(leading, axis, down)  21.7 us
    slice x10, local copies, waits for them, and re-layouts, padded_2(): last = lax.slice_in_dim(array, length - width, length, axis=dim)  12.3 us
    concatenate x9, other arithmetic, padded_2(): array = jnp.concatenate([before, array, after], axis=dim)  10.5 us
  transfers between devices with their start and end apart: 25, of which 21 were waited for; matrix products, arithmetic and copies ran while one was open for 13% of the time, Pallas kernels for 0%

commit v1 on v0

v1 whole, which is shorter than its diff:
```python
import functools

import jax
import jax.numpy as jnp
from jax import lax
from jax.experimental import pallas as pl
from jax.experimental.pallas import tpu as pltpu
from jax.sharding import PartitionSpec as P

H = 8
K = 17
ITERS = 2
MESH = pl.DeviceIdType.MESH
F32 = jnp.float32
BF16 = jnp.bfloat16
NOWHERE = -100000
INV_Y = (0, 2, 1)
ROWS = ((0, 128), (128, 64), (192, 64))


def iota(shape, dim):
    return lax.broadcasted_iota(jnp.int32, shape, dim)


def split(value):
    high = value.astype(BF16)
    low = (value - high.astype(F32)).astype(BF16)
    return high, low


def wide(value):
    high, low = split(value)
    return jnp.concatenate([high, low, high], axis=1)


def tall(value):
    high, low = split(value)
    return jnp.concatenate([high, high, low], axis=0)


def z_place(index):
    return jnp.where(
        index < 128 + H,
        index,
        jnp.where(index < 128 + 2 * H, index - 128 - 2 * H, NOWHERE),
    )


def y_place(index):
    return jnp.where(index < 24, index, index - 32)


def pick(offset, tap):
    total = jnp.zeros(offset.shape, F32)
    for t in range(K):
        total = jnp.where(offset == t, tap(t), total)
    return total


def kernel(
    sizes, psf_ref, extents_ref, views_ref, est_ref, out_ref,
    images, image, forth, back, z_forth, z_back, weights, u_ref, z_ref, z_own, s_ref, sz_ref,
    rc_ref, rz_ref, zc_ref, rz2_ref, view_send, view_recv, send, recv, z_send, z_recv,
):
    n_gx, n_gy, n_gz = sizes
    V = image.shape[0]
    gx, gy, gz = lax.axis_index("gx"), lax.axis_index("gy"), lax.axis_index("gz")
    if n_gx == 2:
        x_targets = (gx, 1 - gx)
        x_exists = (None, None)
        x_offset = (0, H - 2 * H * gx)
        inv_x = (0, 1)
    else:
        x_targets = (gx, gx + 1, gx - 1)
        x_exists = (None, gx < n_gx - 1, gx > 0)
        x_offset = (0, H, -H)
        inv_x = (0, 2, 1)
    slots = len(x_targets)
    y_targets = (gy, gy + 1, gy - 1)
    y_exists = (None, gy < n_gy - 1, gy > 0)
    z_targets = (gz + 1, gz - 1)
    z_exists = (gz < n_gz - 1, gz > 0)
    near = []
    for s in range(slots):
        for y in range(3):
            if s == 0 and y == 0:
                continue
            exists = x_exists[s]
            if y_exists[y] is not None:
                exists = y_exists[y] if exists is None else exists & y_exists[y]
            near.append((s, y, exists, {"gx": x_targets[s], "gy": y_targets[y], "gz": gz}))
    started = []

    def under(exists, do):
        if exists is None:
            do()
        else:
            pl.when(exists)(do)

    def start(exists, make):
        under(exists, lambda: make().start())
        started.append((exists, make))

    def remote(src, dst, s_sem, r_sem, device):
        return lambda: pltpu.make_async_remote_copy(
            src_ref=src, dst_ref=dst, send_sem=s_sem, recv_sem=r_sem,
            device_id=device, device_id_type=MESH,
        )

    barrier = pltpu.get_barrier_semaphore()
    expected = jnp.int32(n_gz - 1)
    for k in range(1, n_gz):
        pl.semaphore_signal(
            barrier, inc=1, device_id={"gx": gx, "gy": gy, "gz": lax.rem(gz + k, n_gz)},
            device_id_type=MESH,
        )
    for s, y, exists, device in near:
        under(exists, functools.partial(
            pl.semaphore_signal, barrier, inc=1, device_id=device, device_id_type=MESH))
        expected = expected + (1 if exists is None else exists.astype(jnp.int32))

    own_views = pltpu.make_async_copy(
        views_ref.at[:, :, :, pl.ds(pl.multiple_of(gz * 128, 128), 128)],
        images.at[gz], view_recv.at[0],
    )
    own_views.start()

    for y in range(16):
        u_ref[0, 0, 8 * y:8 * y + 8, :] = est_ref[:, y, :]
    estimate = u_ref[0, 0, 0:128, :]

    def zero_z(side):
        for it in range(ITERS):
            first = 8 * side
            z_ref[it, 0, 0, first:first + 8, :] = jnp.zeros((8, 128), F32)
            rz2_ref[it, 8 - first:16 - first, :] = jnp.zeros((8, 128), F32)

    for side in range(2):
        pl.when(jnp.logical_not(z_exists[side]))(functools.partial(zero_z, side))

    def zero_near(s, y):
        first, count = ROWS[y]
        for it in range(ITERS):
            u_ref[it, s, first:first + count, :] = jnp.zeros((count, 128), F32)
            z_ref[it, s, y] = jnp.zeros((16, 128), F32)
            rc_ref[it, s, y, 0:count, :] = jnp.zeros((count, 128), F32)
            rz_ref[it, s, y] = jnp.zeros((16, 128), F32)

    for s, y, exists, device in near:
        if exists is not None:
            pl.when(jnp.logical_not(exists))(functools.partial(zero_near, s, y))

    def send_estimate(it, value):
        turned = value.T
        z_own[it, 0:8, :] = turned[0:8]
        z_own[it, 8:16, :] = turned[120:128]
        if it == 0:
            pl.semaphore_wait(barrier, expected)
        for side in (0, 1):
            rows = pl.ds(8 - 8 * side, 8)
            start(z_exists[side], remote(
                z_own.at[it, rows], z_ref.at[it, 0, 0, rows],
                z_send.at[it, 0, side], z_recv.at[it, 0, 1 - side],
                {"gx": gx, "gy": gy, "gz": z_targets[side]}))
        for s, y, exists, device in near:
            source = (0, 64, 0)[y]
            first, count = ROWS[INV_Y[y]]
            start(exists, remote(
                u_ref.at[it, 0, pl.ds(source, count)],
                u_ref.at[it, inv_x[s], pl.ds(first, count)],
                send.at[it, 0, 0, s, y], recv.at[it, 0, 0, inv_x[s], INV_Y[y]], device))

    def pass_z(it):
        for side in (0, 1):
            rows = pl.ds(8 * side, 8)
            under(z_exists[side], lambda rows=rows, side=side: remote(
                z_own.at[it, rows], z_ref.at[it, 0, 0, rows],
                z_send.at[it, 0, side], z_recv.at[it, 0, side],
                {"gx": gx, "gy": gy, "gz": z_targets[side]})().wait_recv())
        for s, y, exists, device in near:
            start(exists, remote(
                z_ref.at[it, 0, 0], z_ref.at[it, inv_x[s], INV_Y[y]],
                send.at[it, 0, 1, s, y], recv.at[it, 0, 1, inv_x[s], INV_Y[y]], device))

    send_estimate(0, estimate)
    for k in range(1, n_gz):
        target = lax.rem(gz + k, n_gz)
        start(None, remote(
            views_ref.at[:, :, :, pl.ds(pl.multiple_of(target * 128, 128), 128)],
            images.at[gz], view_send.at[k], view_recv.at[k],
            {"gx": gx, "gy": gy, "gz": target}))

    def build(v, unused):
        def taps(axis):
            return lambda t: psf_ref[v, axis * K + t]

        scale = jnp.float32(1.0)
        for axis in range(3):
            total = psf_ref[v, axis * K]
            for t in range(1, K):
                total = total + psf_ref[v, axis * K + t]
            scale = scale * total
        inverse = 1.0 / jnp.full((8, 128), scale, F32)
        z_band = pick(z_place(iota((144, 128), 0)) - iota((144, 128), 1) + H, taps(2))
        z_band = z_band * inverse[0:1]
        z_band = jnp.concatenate([z_band, jnp.zeros((112, 128), F32)], axis=0)
        z_forth[v] = tall(z_band)
        z_band_t = jnp.concatenate([z_band[0:128].T, z_band[128:256].T], axis=1)
        z_back[v] = tall(z_band_t)
        lane = iota((16, 256), 1)
        y_rows = pick(y_place(lane // 8) - iota((16, 256), 0) + H, taps(1))
        y_rows_t = pick(y_place(iota((32, 128), 0)) - iota((32, 128), 1) // 8 + H, taps(1))
        row = iota((8, 128), 0)
        column = iota((8, 128), 1) % 8
        for s in range(slots):
            x_tile = pick(x_offset[s] + column - row + H, taps(0))
            x_tile_t = pick(x_offset[s] + row - column + H, taps(0))
            for group in range(2):
                block = y_rows[:, None, 128 * group:128 * group + 128] * x_tile[None]
                high, low = split(block.reshape(128, 128))
                first = s * 256 + group * 128
                width = slots * 256
                forth[v, :, first:first + 128] = high
                forth[v, :, width + first:width + first + 128] = low
                forth[v, :, 2 * width + first:2 * width + first + 128] = high
                block = y_rows_t[16 * group:16 * group + 16, None, :] * x_tile_t[None]
                high, low = split(block.reshape(128, 128))
                back[v, first:first + 128, 0:128] = high
                back[v, first:first + 128, 128:256] = low
                back[v, first:first + 128, 256:384] = high
        z_abs = gz * 128 + z_place(iota((8, 256), 1))
        in_z = (z_abs >= extents_ref[v, 4]) & (z_abs < extents_ref[v, 5])
        z_part = jnp.where(in_z, F32(0.75), F32(0.0))[0:1]
        for s in range(slots):
            rows = iota((256, 128), 0)
            y_abs = gy * 16 + y_place(rows // 8)
            x_abs = gx * 8 + x_offset[s] + rows % 8
            inside = (y_abs >= extents_ref[v, 2]) & (y_abs < extents_ref[v, 3])
            inside = inside & (x_abs >= extents_ref[v, 0]) & (x_abs < extents_ref[v, 1])
            flag = jnp.where(inside, F32(1.0), F32(0.0))
            weights[v, s * 256:s * 256 + 256, 0:128] = flag * z_part[:, 0:128] + 0.25
            weights[v, s * 256:s * 256 + 256, 128:256] = flag * z_part[:, 128:256] + 0.25
        return unused

    pass_z(0)
    lax.fori_loop(0, V, build, 0)
    weight_sum = weights[0, 0:128, 0:128]
    for v in range(1, V):
        weight_sum = weight_sum + weights[v, 0:128, 0:128]

    half = iota((16, 128), 1) < 64
    for it in range(ITERS):
        for s, y, exists, device in near:
            first, count = ROWS[y]
            under(exists, lambda s=s, y=y, first=first, count=count, device=device: remote(
                u_ref.at[it, s, pl.ds(first, count)], u_ref.at[it, s, pl.ds(first, count)],
                send.at[it, 0, 0, s, y], recv.at[it, 0, 0, s, y], device)().wait_recv())
        for s, y, exists, device in near:
            under(exists, lambda s=s, y=y, device=device: remote(
                z_ref.at[it, s, y], z_ref.at[it, s, y],
                send.at[it, 0, 1, s, y], recv.at[it, 0, 1, s, y], device)().wait_recv())
        pieces = []
        fill = jnp.zeros((112, 128), F32)
        for s in range(slots):
            halo = jnp.where(half, z_ref[it, s, 1], z_ref[it, s, 2])
            for group, strip in enumerate((z_ref[it, s, 0], halo)):
                turned = jnp.concatenate([strip, fill], axis=0).T
                middle = u_ref[it, s, 128 * group:128 * group + 128, :]
                pieces.append(jnp.concatenate([middle, turned], axis=1))
        padded = tall(jnp.concatenate(pieces, axis=0))
        blurred = []
        for v in range(V):
            across = jnp.dot(forth[v], padded, preferred_element_type=F32)
            blurred.append(jnp.dot(wide(across), z_forth[v], preferred_element_type=F32))
        if it == 0:
            own_views.wait()
            for k in range(1, n_gz):
                remote(
                    images.at[0], images.at[lax.rem(gz + n_gz - k, n_gz)],
                    view_send.at[k], view_recv.at[k],
                    {"gx": gx, "gy": gy, "gz": lax.rem(gz + n_gz - k, n_gz)})().wait_recv()
            per = 16 // n_gz
            for v in range(V):
                for g in range(n_gz):
                    for yy in range(per):
                        first = 8 * (per * g + yy)
                        image[v, first:first + 8, :] = images[g, v, :, yy, :]
        spread = []
        for v in range(V):
            ratio = image[v] / blurred[v]
            lines = jnp.dot(wide(ratio), z_back[v], preferred_element_type=F32)
            spread.append(tall(lines))

        def summed(first):
            total = None
            for v in range(V):
                part = jnp.dot(
                    back[v, first:first + 128, :], spread[v], preferred_element_type=F32)
                part = part * weights[v, first:first + 128, :]
                total = part if total is None else total + part
            return total

        for s in range(slots - 1, -1, -1):
            for group in (1, 0):
                total = summed(s * 256 + group * 128)
                if s == 0 and group == 0:
                    own_total = total[:, 0:128]
                    own_z = total[:, 128:256].T[0:16]
                    continue
                s_ref[it, s, 128 * group:128 * group + 128, :] = total[:, 0:128]
                sz_ref[it, s, group] = total[:, 128:256].T[0:16]
                for t, y, exists, device in near:
                    if t != s or (y > 0) != (group == 1):
                        continue
                    first, count = ROWS[y]
                    start(exists, remote(
                        sz_ref.at[it, s, group], rz_ref.at[it, inv_x[s], INV_Y[y]],
                        send.at[it, 1, 1, s, y], recv.at[it, 1, 1, inv_x[s], INV_Y[y]], device))
                    start(exists, remote(
                        s_ref.at[it, s, pl.ds(first, count)],
                        rc_ref.at[it, inv_x[s], INV_Y[y], pl.ds(0, count)],
                        send.at[it, 1, 0, s, y], recv.at[it, 1, 0, inv_x[s], INV_Y[y]], device))
        for s, y, exists, device in near:
            under(exists, lambda s=s, y=y, device=device: remote(
                rz_ref.at[it, s, y], rz_ref.at[it, s, y],
                send.at[it, 1, 1, s, y], recv.at[it, 1, 1, s, y], device)().wait_recv())
        for s in range(slots):
            if s > 0:
                own_z = own_z + rz_ref[it, s, 0]
            own_z = own_z + jnp.where(half, rz_ref[it, s, 2], rz_ref[it, s, 1])
        zc_ref[it] = own_z
        for side in (0, 1):
            rows = pl.ds(8 * side, 8)
            start(z_exists[side], remote(
                zc_ref.at[it, rows], rz2_ref.at[it, rows],
                z_send.at[it, 1, side], z_recv.at[it, 1, side],
                {"gx": gx, "gy": gy, "gz": z_targets[side]}))
        for s, y, exists, device in near:
            count = ROWS[y][1]
            under(exists, lambda s=s, y=y, count=count, device=device: remote(
                rc_ref.at[it, s, y, pl.ds(0, count)], rc_ref.at[it, s, y, pl.ds(0, count)],
                send.at[it, 1, 0, s, y], recv.at[it, 1, 0, s, y], device)().wait_recv())
        for s in range(slots):
            if s > 0:
                own_total = own_total + rc_ref[it, s, 0]
            own_total = own_total + jnp.concatenate(
                [rc_ref[it, s, 2, 0:64, :], rc_ref[it, s, 1, 0:64, :]], axis=0)
        for side in (0, 1):
            rows = pl.ds(8 * side, 8)
            under(z_exists[1 - side], lambda rows=rows, side=side: remote(
                zc_ref.at[it, rows], rz2_ref.at[it, rows],
                z_send.at[it, 1, side], z_recv.at[it, 1, side],
                {"gx": gx, "gy": gy, "gz": z_targets[1 - side]})().wait_recv())
        edge = jnp.concatenate(
            [rz2_ref[it, 0:8, :], jnp.zeros((112, 128), F32), rz2_ref[it, 8:16, :]], axis=0)
        own_total = own_total + edge.T
        estimate = estimate * (own_total / weight_sum)
        if it < ITERS - 1:
            u_ref[it + 1, 0, 0:128, :] = estimate
            send_estimate(it + 1, estimate)
            pass_z(it + 1)
    for y in range(16):
        out_ref[:, y, :] = estimate[8 * y:8 * y + 8, :]
    for exists, make in started:
        under(exists, lambda make=make: make().wait_send())


def shards(sizes, views, estimate, psf, extents):
    n_gx, n_gy, n_gz = sizes
    V = views.shape[0]
    slots = 2 if n_gx == 2 else 3
    rows = slots * 256
    smem = pl.BlockSpec(memory_space=pltpu.SMEM)
    vmem = pl.BlockSpec(memory_space=pltpu.VMEM)
    return pl.pallas_call(
        functools.partial(kernel, sizes),
        out_shape=jax.ShapeDtypeStruct(estimate.shape, F32),
        in_specs=[smem, smem, pl.BlockSpec(memory_space=pl.ANY), vmem],
        out_specs=vmem,
        scratch_shapes=[
            pltpu.VMEM((n_gz,) + views.shape[:3] + (128,), F32),
            pltpu.VMEM((V, 128, 128), F32),
            pltpu.VMEM((V, 128, 3 * rows), BF16),
            pltpu.VMEM((V, rows, 384), BF16),
            pltpu.VMEM((V, 768, 128), BF16),
            pltpu.VMEM((V, 384, 256), BF16),
            pltpu.VMEM((V, rows, 256), F32),
            pltpu.VMEM((ITERS, slots, 256, 128), F32),
            pltpu.VMEM((ITERS, slots, 3, 16, 128), F32),
            pltpu.VMEM((ITERS, 16, 128), F32),
            pltpu.VMEM((ITERS, slots, 256, 128), F32),
            pltpu.VMEM((ITERS, slots, 2, 16, 128), F32),
            pltpu.VMEM((ITERS, slots, 3, 128, 128), F32),
            pltpu.VMEM((ITERS, slots, 3, 16, 128), F32),
            pltpu.VMEM((ITERS, 16, 128), F32),
            pltpu.VMEM((ITERS, 16, 128), F32),
            pltpu.SemaphoreType.DMA((n_gz,)),
            pltpu.SemaphoreType.DMA((n_gz,)),
            pltpu.SemaphoreType.DMA((ITERS, 2, 2, slots, 3)),
            pltpu.SemaphoreType.DMA((ITERS, 2, 2, slots, 3)),
            pltpu.SemaphoreType.DMA((ITERS, 2, 2)),
            pltpu.SemaphoreType.DMA((ITERS, 2, 2)),
        ],
        compiler_params=pltpu.CompilerParams(
            collective_id=0, has_side_effects=True, vmem_limit_bytes=40 * 1024 * 1024
        ),
    )(psf.reshape(V, 3 * K), extents.reshape(V, 6), views, estimate)


def solution(mesh):
    sizes = (mesh.shape["gx"], mesh.shape["gy"], mesh.shape["gz"])
    placed = (P(None, "gx", ("gy", "gz"), None), P("gx", "gy", "gz"), P(), P())
    return jax.shard_map(
        functools.partial(shards, sizes), mesh=mesh, in_specs=placed,
        out_specs=P("gx", "gy", "gz"), check_vma=False,
    )
```

time: 242 us -> 38.8 us (0.16); the launches traced: 237 us -> 38.6 us
  waiting for transfers between devices: 74 us -> 0 us
  starting transfers between devices: 60.9 us -> 0 us
  local copies, waits for them, and re-layouts: 61.1 us -> 3.37 us
  Pallas kernels: 0 us -> 35.2 us
  matrix products: 27 us -> 0 us
  other arithmetic: 13 us -> 0 us
    ppermute x24 -> x0, waiting for transfers between devices: 74 us -> none  [the longest x12 44.1 us: padded_2(): after = lax.ppermute(leading, axis, down)]
    ppermute x24 -> x0, starting transfers between devices: 56.5 us -> none  [the longest x12 34.8 us: padded_2(): before = lax.ppermute(last, axis, up)]
    pallas_call x0 -> x1, Pallas kernels: none -> 35.2 us  [shards(): pl.pallas_call(functools.partial(kernel, sizes), out_shape=jax.ShapeDtype...]
    dot_general x18 -> x0, matrix products: 27 us -> none  [the longest x12 23.3 us: blur_along(): return jnp.einsum(form, padded, matrix, precision=lax.Precision.HIGHEST)]
    unnamed x66 -> x7, local copies, waits for them, and re-layouts: 28.1 us -> 2.47 us
    slice x16 -> x0, local copies, waits for them, and re-layouts: 16.7 us -> none  [the longest x10 12.3 us: padded_2(): last = lax.slice_in_dim(array, length - width, length, axis=dim)]
    concatenate x9 -> x0, other arithmetic: 10.5 us -> none  [padded_2(): array = jnp.concatenate([before, array, after], axis=dim)]
    ppermute x4 -> x0, local copies, waits for them, and re-layouts: 9.95 us -> none  [the longest x2 6.44 us: padded_2(): after = lax.ppermute(leading, axis, down)]
  transfers between devices with their start and end apart: 25 -> 0, of which waited for: 21 -> 0; matrix products, arithmetic and copies ran while one was open for 13% -> 0% of each run, Pallas kernels for 0% -> 0%
where the time goes in v1:
time: 38.8 us; the launch traced here: 38.6 us
  Pallas kernels  35.2 us (91%)
  local copies, waits for them, and re-layouts  3.37 us (9%)
    pallas_call x1, Pallas kernels, shards(): pl.pallas_call(functools.partial(kernel, sizes), out_shape=jax.ShapeDtype...  35.2 us
    unnamed x7, local copies, waits for them, and re-layouts  2.47 us
    reshape x1, local copies, waits for them, and re-layouts, shards(): psf.reshape(V, 3 * K)  0.8 us

profile of v1, /device:TPU:1, one launch (start us, length us, event | category | flops | bytes accessed | tf_op | source)
XLA Modules:
  0.0 38.6 jit_solution(4476809408588568835)
XLA Ops:
  0.0 0.0 copy-start.2
  0.0 0.8 %reshape.6.psf_ref = f32[6,51]{1,0:T(8,128)S(1)} reshape(f32[6,3,17]{2,1,0:T(4,128)} %param.6) | data formatting | bytes 2448 | tf_op jit(solution)/shard_map/reshape | solution.py:407
  0.8 0.0 copy-done.2
  0.8 0.1 copy.5.extents_ref
  0.9 0.0 copy-start
  0.9 1.0 %copy-done = f32[6,8,4,512]{3,2,1,0:T(4,128)S(1)} copy-done((f32[6,8,4,512]{3,2,1,0:T(4,128)S(1)}, f32[6,8,4,512]{3,2,1,0:T(4,128)}, u32[]{:S(2)}) %copy-start) | copy-done | bytes 393240
  1.9 0.0 copy-start.1
  1.9 0.8 %copy-done.1 = f32[8,16,128]{2,1,0:T(8,128)S(1)} copy-done((f32[8,16,128]{2,1,0:T(8,128)S(1)}, f32[8,16,128]{2,1,0:T(8,128)}, u32[]{:S(2)}) %copy-start.1) | copy-done | bytes 65560
  2.7 35.2 %shard_map.46 = f32[8,16,128]{2,1,0:T(8,128)S(1)} custom-call(f32[6,51]{1,0:T(8,128)S(1)} %reshape.6.psf_ref, s32[6,6]{1,0:T(8,128)S(1)} %copy.5.extents_ref, f32[6,8,4,512]{3,2,1,0:T(4,128)S(1)} %copy-done, f32[8,16,128]{2,1,0:T(8,128)S(1)} %copy-done.1), custom_call_target="tpu_custom_call" | custom-call | tf_op jit(solution)/shard_map/pallas_call | solution.py:375
  38.0 0.6 %copy.7 = f32[8,16,128]{2,1,0:T(8,128)} copy(f32[8,16,128]{2,1,0:T(8,128)S(1)} %shard_map.46) | data formatting | bytes 131072
  (1 shorter events, 0.0 us)
Async XLA Ops:
  0.0 0.8 %copy-start.2 = (s32[6,3,2]{0,2,1:T(2,128)S(1)}, s32[6,3,2]{0,2,1:T(2,128)}, u32[]{:S(2)}) copy-start(s32[6,3,2]{0,2,1:T(2,128)} %param.7) | copy-start | bytes 436
  0.9 1.0 %copy-start = (f32[6,8,4,512]{3,2,1,0:T(4,128)S(1)}, f32[6,8,4,512]{3,2,1,0:T(4,128)}, u32[]{:S(2)}) copy-start(f32[6,8,4,512]{3,2,1,0:T(4,128)} %views_ref.1) | copy-start | bytes 1179652
  1.9 0.8 %copy-start.1 = (f32[8,16,128]{2,1,0:T(8,128)S(1)}, f32[8,16,128]{2,1,0:T(8,128)}, u32[]{:S(2)}) copy-start(f32[8,16,128]{2,1,0:T(8,128)} %est_ref.1) | copy-start | bytes 196612

commit v2 on v1

--- a/solution.py
+++ b/solution.py
@@ -59,8 +59,8 @@
 
 def kernel(
     sizes, psf_ref, extents_ref, views_ref, est_ref, out_ref,
-    images, image, forth, back, z_forth, z_back, weights, u_ref, z_ref, z_own, s_ref, sz_ref,
-    rc_ref, rz_ref, zc_ref, rz2_ref, view_send, view_recv, send, recv, z_send, z_recv,
+    est_in, images, image, forth, back, z_forth, z_back, weights, u_ref, z_ref, z_own, s_ref, sz_ref,
+    rc_ref, rz_ref, zc_ref, rz2_ref, est_sem, view_send, view_recv, send, recv, z_send, z_recv,
 ):
     n_gx, n_gy, n_gz = sizes
     V = image.shape[0]
@@ -107,6 +107,8 @@
             device_id=device, device_id_type=MESH,
         )
 
+    est_copy = pltpu.make_async_copy(est_ref, est_in, est_sem)
+    est_copy.start()
     barrier = pltpu.get_barrier_semaphore()
     expected = jnp.int32(n_gz - 1)
     for k in range(1, n_gz):
@@ -125,10 +127,6 @@
     )
     own_views.start()
 
-    for y in range(16):
-        u_ref[0, 0, 8 * y:8 * y + 8, :] = est_ref[:, y, :]
-    estimate = u_ref[0, 0, 0:128, :]
-
     def zero_z(side):
         for it in range(ITERS):
             first = 8 * side
@@ -149,6 +147,11 @@
     for s, y, exists, device in near:
         if exists is not None:
             pl.when(jnp.logical_not(exists))(functools.partial(zero_near, s, y))
+
+    est_copy.wait()
+    for y in range(16):
+        u_ref[0, 0, 8 * y:8 * y + 8, :] = est_in[:, y, :]
+    estimate = u_ref[0, 0, 0:128, :]
 
     def send_estimate(it, value):
         turned = value.T
@@ -192,13 +195,13 @@
 
     def build(v, unused):
         def taps(axis):
-            return lambda t: psf_ref[v, axis * K + t]
+            return lambda t: psf_ref[v, axis, t]
 
         scale = jnp.float32(1.0)
         for axis in range(3):
-            total = psf_ref[v, axis * K]
+            total = psf_ref[v, axis, 0]
             for t in range(1, K):
-                total = total + psf_ref[v, axis * K + t]
+                total = total + psf_ref[v, axis, t]
             scale = scale * total
         inverse = 1.0 / jnp.full((8, 128), scale, F32)
         z_band = pick(z_place(iota((144, 128), 0)) - iota((144, 128), 1) + H, taps(2))
@@ -207,6 +210,7 @@
         z_forth[v] = tall(z_band)
         z_band_t = jnp.concatenate([z_band[0:128].T, z_band[128:256].T], axis=1)
         z_back[v] = tall(z_band_t)
+        own = pl.ds(pl.multiple_of(v * 128, 128), 128)
         lane = iota((16, 256), 1)
         y_rows = pick(y_place(lane // 8) - iota((16, 256), 0) + H, taps(1))
         y_rows_t = pick(y_place(iota((32, 128), 0)) - iota((32, 128), 1) // 8 + H, taps(1))
@@ -220,30 +224,31 @@
                 high, low = split(block.reshape(128, 128))
                 first = s * 256 + group * 128
                 width = slots * 256
-                forth[v, :, first:first + 128] = high
-                forth[v, :, width + first:width + first + 128] = low
-                forth[v, :, 2 * width + first:2 * width + first + 128] = high
+                forth[own, first:first + 128] = high
+                forth[own, width + first:width + first + 128] = low
+                forth[own, 2 * width + first:2 * width + first + 128] = high
                 block = y_rows_t[16 * group:16 * group + 16, None, :] * x_tile_t[None]
                 high, low = split(block.reshape(128, 128))
                 back[v, first:first + 128, 0:128] = high
                 back[v, first:first + 128, 128:256] = low
                 back[v, first:first + 128, 256:384] = high
         z_abs = gz * 128 + z_place(iota((8, 256), 1))
-        in_z = (z_abs >= extents_ref[v, 4]) & (z_abs < extents_ref[v, 5])
+        in_z = (z_abs >= extents_ref[v, 2, 0]) & (z_abs < extents_ref[v, 2, 1])
         z_part = jnp.where(in_z, F32(0.75), F32(0.0))[0:1]
         for s in range(slots):
             rows = iota((256, 128), 0)
             y_abs = gy * 16 + y_place(rows // 8)
             x_abs = gx * 8 + x_offset[s] + rows % 8
-            inside = (y_abs >= extents_ref[v, 2]) & (y_abs < extents_ref[v, 3])
-            inside = inside & (x_abs >= extents_ref[v, 0]) & (x_abs < extents_ref[v, 1])
+            inside = (y_abs >= extents_ref[v, 1, 0]) & (y_abs < extents_ref[v, 1, 1])
+            inside = inside & (x_abs >= extents_ref[v, 0, 0]) & (x_abs < extents_ref[v, 0, 1])
             flag = jnp.where(inside, F32(1.0), F32(0.0))
             weights[v, s * 256:s * 256 + 256, 0:128] = flag * z_part[:, 0:128] + 0.25
             weights[v, s * 256:s * 256 + 256, 128:256] = flag * z_part[:, 128:256] + 0.25
         return unused
 
+    lax.fori_loop(0, 2, build, 0)
     pass_z(0)
-    lax.fori_loop(0, V, build, 0)
+    lax.fori_loop(2, V, build, 0)
     weight_sum = weights[0, 0:128, 0:128]
     for v in range(1, V):
         weight_sum = weight_sum + weights[v, 0:128, 0:128]
@@ -269,9 +274,10 @@
                 pieces.append(jnp.concatenate([middle, turned], axis=1))
         padded = tall(jnp.concatenate(pieces, axis=0))
         blurred = []
+        across = jnp.dot(forth[...], padded, preferred_element_type=F32)
         for v in range(V):
-            across = jnp.dot(forth[v], padded, preferred_element_type=F32)
-            blurred.append(jnp.dot(wide(across), z_forth[v], preferred_element_type=F32))
+            lines = wide(across[128 * v:128 * v + 128])
+            blurred.append(jnp.dot(lines, z_forth[v], preferred_element_type=F32))
         if it == 0:
             own_views.wait()
             for k in range(1, n_gz):
@@ -295,14 +301,15 @@
             total = None
             for v in range(V):
                 part = jnp.dot(
-                    back[v, first:first + 128, :], spread[v], preferred_element_type=F32)
-                part = part * weights[v, first:first + 128, :]
+                    back[v, first:first + 256, :], spread[v], preferred_element_type=F32)
+                part = part * weights[v, first:first + 256, :]
                 total = part if total is None else total + part
             return total
 
         for s in range(slots - 1, -1, -1):
+            both = summed(s * 256)
             for group in (1, 0):
-                total = summed(s * 256 + group * 128)
+                total = both[128 * group:128 * group + 128]
                 if s == 0 and group == 0:
                     own_total = total[:, 0:128]
                     own_z = total[:, 128:256].T[0:16]
@@ -372,15 +379,17 @@
     rows = slots * 256
     smem = pl.BlockSpec(memory_space=pltpu.SMEM)
     vmem = pl.BlockSpec(memory_space=pltpu.VMEM)
+    whole = pl.BlockSpec(memory_space=pl.ANY)
     return pl.pallas_call(
         functools.partial(kernel, sizes),
         out_shape=jax.ShapeDtypeStruct(estimate.shape, F32),
-        in_specs=[smem, smem, pl.BlockSpec(memory_space=pl.ANY), vmem],
+        in_specs=[smem, smem, whole, whole],
         out_specs=vmem,
         scratch_shapes=[
+            pltpu.VMEM(estimate.shape, F32),
             pltpu.VMEM((n_gz,) + views.shape[:3] + (128,), F32),
             pltpu.VMEM((V, 128, 128), F32),
-            pltpu.VMEM((V, 128, 3 * rows), BF16),
+            pltpu.VMEM((V * 128, 3 * rows), BF16),
             pltpu.VMEM((V, rows, 384), BF16),
             pltpu.VMEM((V, 768, 128), BF16),
             pltpu.VMEM((V, 384, 256), BF16),
@@ -394,6 +403,7 @@
             pltpu.VMEM((ITERS, slots, 3, 16, 128), F32),
             pltpu.VMEM((ITERS, 16, 128), F32),
             pltpu.VMEM((ITERS, 16, 128), F32),
+            pltpu.SemaphoreType.DMA,
             pltpu.SemaphoreType.DMA((n_gz,)),
             pltpu.SemaphoreType.DMA((n_gz,)),
             pltpu.SemaphoreType.DMA((ITERS, 2, 2, slots, 3)),
@@ -402,9 +412,9 @@
             pltpu.SemaphoreType.DMA((ITERS, 2, 2)),
         ],
         compiler_params=pltpu.CompilerParams(
-            collective_id=0, has_side_effects=True, vmem_limit_bytes=40 * 1024 * 1024
+            collective_id=0, has_side_effects=True, vmem_limit_bytes=60 * 1024 * 1024
         ),
-    )(psf.reshape(V, 3 * K), extents.reshape(V, 6), views, estimate)
+    )(psf, extents, views, estimate)
 
 
 def solution(mesh):

time: 38.8 us -> 39.1 us (level)
  Pallas kernels: 35.2 us -> 35.9 us
  local copies, waits for them, and re-layouts: 3.37 us -> 2.85 us
    reshape x3 -> x0, local copies, waits for them, and re-layouts: 0.9 us -> none  [the longest x1 0.8 us: shards(): psf.reshape(V, 3 * K)]
    pallas_call x1, Pallas kernels: 35.2 us -> 35.9 us  [shards(): pl.pallas_call(functools.partial(kernel, sizes), out_shape=jax.ShapeDtype...]
    unnamed x7 -> x2, local copies, waits for them, and re-layouts: 2.47 us -> 2.85 us
where the time goes in v2:
time: 39.1 us; the launch traced here: 38.8 us
  Pallas kernels  35.9 us (92%)
  local copies, waits for them, and re-layouts  2.85 us (7%)
    pallas_call x1, Pallas kernels, shards(): pl.pallas_call(functools.partial(kernel, sizes), out_shape=jax.ShapeDtype...  35.9 us
    unnamed x2, local copies, waits for them, and re-layouts  2.85 us

profile of v2, /device:TPU:1, one launch (start us, length us, event | category | flops | bytes accessed | tf_op | source)
XLA Modules:
  0.0 38.8 jit_solution(16282487653252700709)
XLA Ops:
  0.0 1.4 %copy.5.extents_ref = s32[6,3,2]{2,1,0:T(4,128)} copy(s32[6,3,2]{0,2,1:T(2,128)} %param.7) | data formatting | bytes 288 | tf_op args[3]
  1.4 35.9 %shard_map.46 = f32[8,16,128]{2,1,0:T(8,128)} custom-call(f32[6,3,17]{2,1,0:T(4,128)} %psf_ref.1, s32[6,3,2]{2,1,0:T(4,128)} %copy.5.extents_ref, f32[6,8,4,512]{3,2,1,0:T(4,128)} %views_ref.1, f32[8,16,128]{2,1,0:T(8,128)} %est_ref.1), custom_call_target="tpu_custom_call" | custom-call | tf_op jit(solution)/shard_map/pallas_call | solution.py:383
  37.3 1.5 %copy.7 = f32[8,16,128]{2,1,0:T(8,128)} copy(f32[8,16,128]{2,1,0:T(8,128)} %shard_map.46) | data formatting | bytes 131072

commit v3 on v2

--- a/solution.py
+++ b/solution.py
@@ -60,7 +60,7 @@
 def kernel(
     sizes, psf_ref, extents_ref, views_ref, est_ref, out_ref,
     est_in, images, image, forth, back, z_forth, z_back, weights, u_ref, z_ref, z_own, s_ref, sz_ref,
-    rc_ref, rz_ref, zc_ref, rz2_ref, est_sem, view_send, view_recv, send, recv, z_send, z_recv,
+    rc_ref, rz_ref, est_sem, view_send, view_recv, send, recv, z_send, z_recv,
 ):
     n_gx, n_gy, n_gz = sizes
     V = image.shape[0]
@@ -89,6 +89,16 @@
             if y_exists[y] is not None:
                 exists = y_exists[y] if exists is None else exists & y_exists[y]
             near.append((s, y, exists, {"gx": x_targets[s], "gy": y_targets[y], "gz": gz}))
+    side_near = []
+    for s in range(slots):
+        for y in range(3):
+            for side in range(2):
+                exists = z_exists[side]
+                for other in (x_exists[s], y_exists[y]):
+                    if other is not None:
+                        exists = exists & other
+                device = {"gx": x_targets[s], "gy": y_targets[y], "gz": z_targets[side]}
+                side_near.append((s, y, side, exists, device))
     started = []
 
     def under(exists, do):
@@ -111,6 +121,12 @@
     est_copy.start()
     barrier = pltpu.get_barrier_semaphore()
     expected = jnp.int32(n_gz - 1)
+    for s, y, side, exists, device in side_near:
+        if s == 0 and y == 0:
+            continue
+        under(exists, functools.partial(
+            pl.semaphore_signal, barrier, inc=1, device_id=device, device_id_type=MESH))
+        expected = expected + exists.astype(jnp.int32)
     for k in range(1, n_gz):
         pl.semaphore_signal(
             barrier, inc=1, device_id={"gx": gx, "gy": gy, "gz": lax.rem(gz + k, n_gz)},
@@ -127,22 +143,20 @@
     )
     own_views.start()
 
-    def zero_z(side):
+    def zero_side(s, y, side):
+        first = 8 * side
         for it in range(ITERS):
-            first = 8 * side
-            z_ref[it, 0, 0, first:first + 8, :] = jnp.zeros((8, 128), F32)
-            rz2_ref[it, 8 - first:16 - first, :] = jnp.zeros((8, 128), F32)
-
-    for side in range(2):
-        pl.when(jnp.logical_not(z_exists[side]))(functools.partial(zero_z, side))
+            z_ref[it, s, y, first:first + 8, :] = jnp.zeros((8, 128), F32)
+            rz_ref[it, s, y, 8 - first:16 - first, :] = jnp.zeros((8, 128), F32)
+
+    for s, y, side, exists, device in side_near:
+        pl.when(jnp.logical_not(exists))(functools.partial(zero_side, s, y, side))
 
     def zero_near(s, y):
         first, count = ROWS[y]
         for it in range(ITERS):
             u_ref[it, s, first:first + count, :] = jnp.zeros((count, 128), F32)
-            z_ref[it, s, y] = jnp.zeros((16, 128), F32)
             rc_ref[it, s, y, 0:count, :] = jnp.zeros((count, 128), F32)
-            rz_ref[it, s, y] = jnp.zeros((16, 128), F32)
 
     for s, y, exists, device in near:
         if exists is not None:
@@ -154,36 +168,24 @@
     estimate = u_ref[0, 0, 0:128, :]
 
     def send_estimate(it, value):
-        turned = value.T
-        z_own[it, 0:8, :] = turned[0:8]
-        z_own[it, 8:16, :] = turned[120:128]
         if it == 0:
             pl.semaphore_wait(barrier, expected)
-        for side in (0, 1):
-            rows = pl.ds(8 - 8 * side, 8)
-            start(z_exists[side], remote(
-                z_own.at[it, rows], z_ref.at[it, 0, 0, rows],
-                z_send.at[it, 0, side], z_recv.at[it, 0, 1 - side],
-                {"gx": gx, "gy": gy, "gz": z_targets[side]}))
-        for s, y, exists, device in near:
+        for s, y, exists, device in near[::-1]:
             source = (0, 64, 0)[y]
             first, count = ROWS[INV_Y[y]]
             start(exists, remote(
                 u_ref.at[it, 0, pl.ds(source, count)],
                 u_ref.at[it, inv_x[s], pl.ds(first, count)],
-                send.at[it, 0, 0, s, y], recv.at[it, 0, 0, inv_x[s], INV_Y[y]], device))
-
-    def pass_z(it):
-        for side in (0, 1):
-            rows = pl.ds(8 * side, 8)
-            under(z_exists[side], lambda rows=rows, side=side: remote(
-                z_own.at[it, rows], z_ref.at[it, 0, 0, rows],
-                z_send.at[it, 0, side], z_recv.at[it, 0, side],
-                {"gx": gx, "gy": gy, "gz": z_targets[side]})().wait_recv())
-        for s, y, exists, device in near:
+                send.at[it, 0, s, y], recv.at[it, 0, inv_x[s], INV_Y[y]], device))
+        turned = value.T
+        z_own[it, 0:8, :] = turned[0:8]
+        z_own[it, 8:16, :] = turned[120:128]
+        for s, y, side, exists, device in side_near[::-1]:
+            rows = pl.ds(8 - 8 * side, 8)
             start(exists, remote(
-                z_ref.at[it, 0, 0], z_ref.at[it, inv_x[s], INV_Y[y]],
-                send.at[it, 0, 1, s, y], recv.at[it, 0, 1, inv_x[s], INV_Y[y]], device))
+                z_own.at[it, rows], z_ref.at[it, inv_x[s], INV_Y[y], rows],
+                z_send.at[it, 0, s, y, side], z_recv.at[it, 0, inv_x[s], INV_Y[y], 1 - side],
+                device))
 
     send_estimate(0, estimate)
     for k in range(1, n_gz):
@@ -233,22 +235,20 @@
                 back[v, first:first + 128, 128:256] = low
                 back[v, first:first + 128, 256:384] = high
         z_abs = gz * 128 + z_place(iota((8, 256), 1))
-        in_z = (z_abs >= extents_ref[v, 2, 0]) & (z_abs < extents_ref[v, 2, 1])
+        in_z = (z_abs >= extents_ref[2, 0, v]) & (z_abs < extents_ref[2, 1, v])
         z_part = jnp.where(in_z, F32(0.75), F32(0.0))[0:1]
         for s in range(slots):
             rows = iota((256, 128), 0)
             y_abs = gy * 16 + y_place(rows // 8)
             x_abs = gx * 8 + x_offset[s] + rows % 8
-            inside = (y_abs >= extents_ref[v, 1, 0]) & (y_abs < extents_ref[v, 1, 1])
-            inside = inside & (x_abs >= extents_ref[v, 0, 0]) & (x_abs < extents_ref[v, 0, 1])
+            inside = (y_abs >= extents_ref[1, 0, v]) & (y_abs < extents_ref[1, 1, v])
+            inside = inside & (x_abs >= extents_ref[0, 0, v]) & (x_abs < extents_ref[0, 1, v])
             flag = jnp.where(inside, F32(1.0), F32(0.0))
             weights[v, s * 256:s * 256 + 256, 0:128] = flag * z_part[:, 0:128] + 0.25
             weights[v, s * 256:s * 256 + 256, 128:256] = flag * z_part[:, 128:256] + 0.25
         return unused
 
-    lax.fori_loop(0, 2, build, 0)
-    pass_z(0)
-    lax.fori_loop(2, V, build, 0)
+    lax.fori_loop(0, V, build, 0)
     weight_sum = weights[0, 0:128, 0:128]
     for v in range(1, V):
         weight_sum = weight_sum + weights[v, 0:128, 0:128]
@@ -259,11 +259,12 @@
             first, count = ROWS[y]
             under(exists, lambda s=s, y=y, first=first, count=count, device=device: remote(
                 u_ref.at[it, s, pl.ds(first, count)], u_ref.at[it, s, pl.ds(first, count)],
-                send.at[it, 0, 0, s, y], recv.at[it, 0, 0, s, y], device)().wait_recv())
-        for s, y, exists, device in near:
-            under(exists, lambda s=s, y=y, device=device: remote(
-                z_ref.at[it, s, y], z_ref.at[it, s, y],
-                send.at[it, 0, 1, s, y], recv.at[it, 0, 1, s, y], device)().wait_recv())
+                send.at[it, 0, s, y], recv.at[it, 0, s, y], device)().wait_recv())
+        for s, y, side, exists, device in side_near:
+            rows = pl.ds(8 * side, 8)
+            under(exists, lambda s=s, y=y, side=side, rows=rows, device=device: remote(
+                z_own.at[it, rows], z_ref.at[it, s, y, rows],
+                z_send.at[it, 0, s, y, side], z_recv.at[it, 0, s, y, side], device)().wait_recv())
         pieces = []
         fill = jnp.zeros((112, 128), F32)
         for s in range(slots):
@@ -308,64 +309,55 @@
 
         for s in range(slots - 1, -1, -1):
             both = summed(s * 256)
-            for group in (1, 0):
-                total = both[128 * group:128 * group + 128]
-                if s == 0 and group == 0:
-                    own_total = total[:, 0:128]
-                    own_z = total[:, 128:256].T[0:16]
+            if s == 0:
+                own_total = both[0:128, 0:128]
+                s_ref[it, s, 128:256, :] = both[128:256, 0:128]
+            else:
+                s_ref[it, s] = both[:, 0:128]
+            for t, y, exists, device in near:
+                if t != s:
                     continue
-                s_ref[it, s, 128 * group:128 * group + 128, :] = total[:, 0:128]
-                sz_ref[it, s, group] = total[:, 128:256].T[0:16]
-                for t, y, exists, device in near:
-                    if t != s or (y > 0) != (group == 1):
-                        continue
-                    first, count = ROWS[y]
-                    start(exists, remote(
-                        sz_ref.at[it, s, group], rz_ref.at[it, inv_x[s], INV_Y[y]],
-                        send.at[it, 1, 1, s, y], recv.at[it, 1, 1, inv_x[s], INV_Y[y]], device))
-                    start(exists, remote(
-                        s_ref.at[it, s, pl.ds(first, count)],
-                        rc_ref.at[it, inv_x[s], INV_Y[y], pl.ds(0, count)],
-                        send.at[it, 1, 0, s, y], recv.at[it, 1, 0, inv_x[s], INV_Y[y]], device))
-        for s, y, exists, device in near:
-            under(exists, lambda s=s, y=y, device=device: remote(
-                rz_ref.at[it, s, y], rz_ref.at[it, s, y],
-                send.at[it, 1, 1, s, y], recv.at[it, 1, 1, s, y], device)().wait_recv())
+                first, count = ROWS[y]
+                start(exists, remote(
+                    s_ref.at[it, s, pl.ds(first, count)],
+                    rc_ref.at[it, inv_x[s], INV_Y[y], pl.ds(0, count)],
+                    send.at[it, 1, s, y], recv.at[it, 1, inv_x[s], INV_Y[y]], device))
+            for group in (0, 1):
+                sz_ref[it, s, group] = both[128 * group:128 * group + 128, 128:256].T[0:16]
+            for t, y, side, exists, device in side_near:
+                if t != s:
+                    continue
+                rows = pl.ds(8 * side, 8)
+                start(exists, remote(
+                    sz_ref.at[it, s, min(y, 1), rows],
+                    rz_ref.at[it, inv_x[s], INV_Y[y], rows],
+                    z_send.at[it, 1, s, y, side], z_recv.at[it, 1, inv_x[s], INV_Y[y], 1 - side],
+                    device))
+        for s, y, side, exists, device in side_near:
+            rows = pl.ds(8 - 8 * side, 8)
+            under(exists, lambda s=s, y=y, side=side, rows=rows, device=device: remote(
+                sz_ref.at[it, s, 0, rows], rz_ref.at[it, s, y, rows],
+                z_send.at[it, 1, s, y, side], z_recv.at[it, 1, s, y, side], device)().wait_recv())
+        strips = jnp.zeros((16, 128), F32)
         for s in range(slots):
-            if s > 0:
-                own_z = own_z + rz_ref[it, s, 0]
-            own_z = own_z + jnp.where(half, rz_ref[it, s, 2], rz_ref[it, s, 1])
-        zc_ref[it] = own_z
-        for side in (0, 1):
-            rows = pl.ds(8 * side, 8)
-            start(z_exists[side], remote(
-                zc_ref.at[it, rows], rz2_ref.at[it, rows],
-                z_send.at[it, 1, side], z_recv.at[it, 1, side],
-                {"gx": gx, "gy": gy, "gz": z_targets[side]}))
+            strips = strips + rz_ref[it, s, 0]
+            strips = strips + jnp.where(half, rz_ref[it, s, 2], rz_ref[it, s, 1])
+        edge = jnp.concatenate([strips[0:8], jnp.zeros((112, 128), F32), strips[8:16]], axis=0)
+        own_total = own_total + edge.T
         for s, y, exists, device in near:
             count = ROWS[y][1]
             under(exists, lambda s=s, y=y, count=count, device=device: remote(
                 rc_ref.at[it, s, y, pl.ds(0, count)], rc_ref.at[it, s, y, pl.ds(0, count)],
-                send.at[it, 1, 0, s, y], recv.at[it, 1, 0, s, y], device)().wait_recv())
+                send.at[it, 1, s, y], recv.at[it, 1, s, y], device)().wait_recv())
         for s in range(slots):
             if s > 0:
                 own_total = own_total + rc_ref[it, s, 0]
             own_total = own_total + jnp.concatenate(
                 [rc_ref[it, s, 2, 0:64, :], rc_ref[it, s, 1, 0:64, :]], axis=0)
-        for side in (0, 1):
-            rows = pl.ds(8 * side, 8)
-            under(z_exists[1 - side], lambda rows=rows, side=side: remote(
-                zc_ref.at[it, rows], rz2_ref.at[it, rows],
-                z_send.at[it, 1, side], z_recv.at[it, 1, side],
-                {"gx": gx, "gy": gy, "gz": z_targets[1 - side]})().wait_recv())
-        edge = jnp.concatenate(
-            [rz2_ref[it, 0:8, :], jnp.zeros((112, 128), F32), rz2_ref[it, 8:16, :]], axis=0)
-        own_total = own_total + edge.T
         estimate = estimate * (own_total / weight_sum)
         if it < ITERS - 1:
             u_ref[it + 1, 0, 0:128, :] = estimate
             send_estimate(it + 1, estimate)
-            pass_z(it + 1)
     for y in range(16):
         out_ref[:, y, :] = estimate[8 * y:8 * y + 8, :]
     for exists, make in started:
@@ -379,7 +371,7 @@
     rows = slots * 256
     smem = pl.BlockSpec(memory_space=pltpu.SMEM)
     vmem = pl.BlockSpec(memory_space=pltpu.VMEM)
-    whole = pl.BlockSpec(memory_space=pl.ANY)
+    whole = pl.BlockSpec(memory_space=pltpu.HBM)
     return pl.pallas_call(
         functools.partial(kernel, sizes),
         out_shape=jax.ShapeDtypeStruct(estimate.shape, F32),
@@ -401,20 +393,18 @@
             pltpu.VMEM((ITERS, slots, 2, 16, 128), F32),
             pltpu.VMEM((ITERS, slots, 3, 128, 128), F32),
             pltpu.VMEM((ITERS, slots, 3, 16, 128), F32),
-            pltpu.VMEM((ITERS, 16, 128), F32),
-            pltpu.VMEM((ITERS, 16, 128), F32),
             pltpu.SemaphoreType.DMA,
             pltpu.SemaphoreType.DMA((n_gz,)),
             pltpu.SemaphoreType.DMA((n_gz,)),
-            pltpu.SemaphoreType.DMA((ITERS, 2, 2, slots, 3)),
-            pltpu.SemaphoreType.DMA((ITERS, 2, 2, slots, 3)),
-            pltpu.SemaphoreType.DMA((ITERS, 2, 2)),
-            pltpu.SemaphoreType.DMA((ITERS, 2, 2)),
+            pltpu.SemaphoreType.DMA((ITERS, 2, slots, 3)),
+            pltpu.SemaphoreType.DMA((ITERS, 2, slots, 3)),
+            pltpu.SemaphoreType.DMA((ITERS, 2, slots, 3, 2)),
+            pltpu.SemaphoreType.DMA((ITERS, 2, slots, 3, 2)),
         ],
         compiler_params=pltpu.CompilerParams(
             collective_id=0, has_side_effects=True, vmem_limit_bytes=60 * 1024 * 1024
         ),
-    )(psf, extents, views, estimate)
+    )(psf, extents.transpose(1, 2, 0), views, estimate)
 
 
 def solution(mesh):

time: 39.1 us -> 34.4 us (0.88)
  Pallas kernels: 35.9 us -> 32.6 us
  local copies, waits for them, and re-layouts: 2.85 us -> 1.47 us
    pallas_call x1, Pallas kernels: 35.9 us -> 32.6 us  [shards(): pl.pallas_call(functools.partial(kernel, sizes), out_shape=jax.ShapeDtype...]
    unnamed x2 -> x1, local copies, waits for them, and re-layouts: 2.85 us -> 1.47 us
where the time goes in v3:
time: 34.4 us; the launch traced here: 34.1 us
  Pallas kernels  32.6 us (95%)
  local copies, waits for them, and re-layouts  1.47 us (4%)
    pallas_call x1, Pallas kernels, shards(): pl.pallas_call(functools.partial(kernel, sizes), out_shape=jax.ShapeDtype...  32.6 us
    unnamed x1, local copies, waits for them, and re-layouts  1.47 us

profile of v3, /device:TPU:1, one launch (start us, length us, event | category | flops | bytes accessed | tf_op | source)
XLA Modules:
  0.0 34.1 jit_solution(9403578167299357942)
XLA Ops:
  0.0 32.6 %shard_map.46 = f32[8,16,128]{2,1,0:T(8,128)} custom-call(f32[6,3,17]{2,1,0:T(4,128)} %psf_ref.1, s32[3,2,6]{2,1,0:T(2,128)} %bitcast.1, f32[6,8,4,512]{3,2,1,0:T(4,128)} %views_ref.1, f32[8,16,128]{2,1,0:T(8,128)} %est_ref.1), custom_call_target="tpu_custom_call" | custom-call | tf_op jit(solution)/shard_map/pallas_call | solution.py:375
  32.6 1.5 %copy.6 = f32[8,16,128]{2,1,0:T(8,128)} copy(f32[8,16,128]{2,1,0:T(8,128)} %shard_map.46) | data formatting | bytes 131072

commit v4 on v3

--- a/solution.py
+++ b/solution.py
@@ -58,8 +58,8 @@
 
 
 def kernel(
-    sizes, psf_ref, extents_ref, views_ref, est_ref, out_ref,
-    est_in, images, image, forth, back, z_forth, z_back, weights, u_ref, z_ref, z_own, s_ref, sz_ref,
+    sizes, psf_in, extents_in, views_ref, est_ref, out_ref,
+    psf_ref, extents_ref, est_in, images, image, forth, back, z_forth, z_back, weights, u_ref, z_ref, z_own, s_ref, sz_ref,
     rc_ref, rz_ref, est_sem, view_send, view_recv, send, recv, z_send, z_recv,
 ):
     n_gx, n_gy, n_gz = sizes
@@ -111,13 +111,20 @@
         under(exists, lambda: make().start())
         started.append((exists, make))
 
+    def drain():
+        for exists, make in started:
+            under(exists, lambda make=make: make().wait_send())
+        started.clear()
+
     def remote(src, dst, s_sem, r_sem, device):
         return lambda: pltpu.make_async_remote_copy(
             src_ref=src, dst_ref=dst, send_sem=s_sem, recv_sem=r_sem,
             device_id=device, device_id_type=MESH,
         )
 
-    est_copy = pltpu.make_async_copy(est_ref, est_in, est_sem)
+    est_copy = pltpu.make_async_copy(est_ref, est_in, est_sem.at[0])
+    psf_copy = pltpu.make_async_copy(psf_in, psf_ref, est_sem.at[1])
+    extents_copy = pltpu.make_async_copy(extents_in, extents_ref, est_sem.at[2])
     est_copy.start()
     barrier = pltpu.get_barrier_semaphore()
     expected = jnp.int32(n_gz - 1)
@@ -137,6 +144,8 @@
             pl.semaphore_signal, barrier, inc=1, device_id=device, device_id_type=MESH))
         expected = expected + (1 if exists is None else exists.astype(jnp.int32))
 
+    psf_copy.start()
+    extents_copy.start()
     own_views = pltpu.make_async_copy(
         views_ref.at[:, :, :, pl.ds(pl.multiple_of(gz * 128, 128), 128)],
         images.at[gz], view_recv.at[0],
@@ -188,12 +197,17 @@
                 device))
 
     send_estimate(0, estimate)
+    halo_sends = list(started)
+    started.clear()
     for k in range(1, n_gz):
         target = lax.rem(gz + k, n_gz)
         start(None, remote(
             views_ref.at[:, :, :, pl.ds(pl.multiple_of(target * 128, 128), 128)],
             images.at[gz], view_send.at[k], view_recv.at[k],
             {"gx": gx, "gy": gy, "gz": target}))
+
+    view_sends = list(started)
+    started[:] = halo_sends
 
     def build(v, unused):
         def taps(axis):
@@ -248,13 +262,22 @@
             weights[v, s * 256:s * 256 + 256, 128:256] = flag * z_part[:, 128:256] + 0.25
         return unused
 
-    lax.fori_loop(0, V, build, 0)
+    psf_copy.wait()
+    extents_copy.wait()
+
+    def build_pair(i, unused):
+        return build(2 * i + 1, build(2 * i, unused))
+
+    lax.fori_loop(0, V // 2, build_pair, 0)
+    if V % 2:
+        build(V - 1, 0)
     weight_sum = weights[0, 0:128, 0:128]
     for v in range(1, V):
         weight_sum = weight_sum + weights[v, 0:128, 0:128]
 
     half = iota((16, 128), 1) < 64
     for it in range(ITERS):
+        drain()
         for s, y, exists, device in near:
             first, count = ROWS[y]
             under(exists, lambda s=s, y=y, first=first, count=count, device=device: remote(
@@ -333,6 +356,9 @@
                     rz_ref.at[it, inv_x[s], INV_Y[y], rows],
                     z_send.at[it, 1, s, y, side], z_recv.at[it, 1, inv_x[s], INV_Y[y], 1 - side],
                     device))
+        if it == 0:
+            started.extend(view_sends)
+        drain()
         for s, y, side, exists, device in side_near:
             rows = pl.ds(8 - 8 * side, 8)
             under(exists, lambda s=s, y=y, side=side, rows=rows, device=device: remote(
@@ -360,8 +386,6 @@
             send_estimate(it + 1, estimate)
     for y in range(16):
         out_ref[:, y, :] = estimate[8 * y:8 * y + 8, :]
-    for exists, make in started:
-        under(exists, lambda make=make: make().wait_send())
 
 
 def shards(sizes, views, estimate, psf, extents):
@@ -369,15 +393,16 @@
     V = views.shape[0]
     slots = 2 if n_gx == 2 else 3
     rows = slots * 256
-    smem = pl.BlockSpec(memory_space=pltpu.SMEM)
     vmem = pl.BlockSpec(memory_space=pltpu.VMEM)
     whole = pl.BlockSpec(memory_space=pltpu.HBM)
     return pl.pallas_call(
         functools.partial(kernel, sizes),
         out_shape=jax.ShapeDtypeStruct(estimate.shape, F32),
-        in_specs=[smem, smem, whole, whole],
+        in_specs=[whole] * 4,
         out_specs=vmem,
         scratch_shapes=[
+            pltpu.SMEM(psf.shape, F32),
+            pltpu.SMEM((3, 2, V), jnp.int32),
             pltpu.VMEM(estimate.shape, F32),
             pltpu.VMEM((n_gz,) + views.shape[:3] + (128,), F32),
             pltpu.VMEM((V, 128, 128), F32),
@@ -393,7 +418,7 @@
             pltpu.VMEM((ITERS, slots, 2, 16, 128), F32),
             pltpu.VMEM((ITERS, slots, 3, 128, 128), F32),
             pltpu.VMEM((ITERS, slots, 3, 16, 128), F32),
-            pltpu.SemaphoreType.DMA,
+            pltpu.SemaphoreType.DMA((3,)),
             pltpu.SemaphoreType.DMA((n_gz,)),
             pltpu.SemaphoreType.DMA((n_gz,)),
             pltpu.SemaphoreType.DMA((ITERS, 2, slots, 3)),

time: 34.4 us -> 33.3 us (0.968)
  Pallas kernels: 32.6 us -> 31.6 us
    pallas_call x1, Pallas kernels: 32.6 us -> 31.6 us  [shards(): pl.pallas_call(functools.partial(kernel, sizes), out_shape=jax.ShapeDtype...]
where the time goes in v4:
time: 33.3 us; the launch traced here: 33.1 us
  Pallas kernels  31.6 us (95%)
  local copies, waits for them, and re-layouts  1.47 us (4%)
    pallas_call x1, Pallas kernels, shards(): pl.pallas_call(functools.partial(kernel, sizes), out_shape=jax.ShapeDtype...  31.6 us
    unnamed x1, local copies, waits for them, and re-layouts  1.47 us

profile of v4, /device:TPU:1, one launch (start us, length us, event | category | flops | bytes accessed | tf_op | source)
XLA Modules:
  0.0 33.1 jit_solution(10568538271932310369)
XLA Ops:
  0.0 31.6 %shard_map.46 = f32[8,16,128]{2,1,0:T(8,128)} custom-call(f32[6,3,17]{2,1,0:T(4,128)} %psf_in.1, s32[3,2,6]{2,1,0:T(2,128)} %bitcast.1, f32[6,8,4,512]{3,2,1,0:T(4,128)} %views_ref.1, f32[8,16,128]{2,1,0:T(8,128)} %est_ref.1), custom_call_target="tpu_custom_call" | custom-call | tf_op jit(solution)/shard_map/pallas_call | solution.py:398
  31.6 1.5 %copy.6 = f32[8,16,128]{2,1,0:T(8,128)} copy(f32[8,16,128]{2,1,0:T(8,128)} %shard_map.46) | data formatting | bytes 131072

commit v5 on v4

--- a/solution.py
+++ b/solution.py
@@ -265,12 +265,14 @@
     psf_copy.wait()
     extents_copy.wait()
 
-    def build_pair(i, unused):
-        return build(2 * i + 1, build(2 * i, unused))
-
-    lax.fori_loop(0, V // 2, build_pair, 0)
-    if V % 2:
-        build(V - 1, 0)
+    def build_three(i, unused):
+        for k in range(3):
+            unused = build(3 * i + k, unused)
+        return unused
+
+    lax.fori_loop(0, V // 3, build_three, 0)
+    for v in range(V - V % 3, V):
+        build(v, 0)
     weight_sum = weights[0, 0:128, 0:128]
     for v in range(1, V):
         weight_sum = weight_sum + weights[v, 0:128, 0:128]

time: 33.3 us -> 33.3 us (level)
  no operation moved by 1% of the time
where the time goes in v5:
time: 33.3 us; the launch traced here: 33.1 us
  Pallas kernels  31.6 us (95%)
  local copies, waits for them, and re-layouts  1.47 us (4%)
    pallas_call x1, Pallas kernels, shards(): pl.pallas_call(functools.partial(kernel, sizes), out_shape=jax.ShapeDtype...  31.6 us
    unnamed x1, local copies, waits for them, and re-layouts  1.47 us

profile of v5, /device:TPU:1, one launch (start us, length us, event | category | flops | bytes accessed | tf_op | source)
XLA Modules:
  0.0 33.1 jit_solution(862845899630332998)
XLA Ops:
  0.0 31.6 %shard_map.46 = f32[8,16,128]{2,1,0:T(8,128)} custom-call(f32[6,3,17]{2,1,0:T(4,128)} %psf_in.1, s32[3,2,6]{2,1,0:T(2,128)} %bitcast.1, f32[6,8,4,512]{3,2,1,0:T(4,128)} %views_ref.1, f32[8,16,128]{2,1,0:T(8,128)} %est_ref.1), custom_call_target="tpu_custom_call" | custom-call | tf_op jit(solution)/shard_map/pallas_call | solution.py:400
  31.6 1.5 %copy.6 = f32[8,16,128]{2,1,0:T(8,128)} copy(f32[8,16,128]{2,1,0:T(8,128)} %shard_map.46) | data formatting | bytes 131072
